TPU v7x, 256 devices: a whole 4x4x8 slice. The times are simulated.
256 devices in a mesh: gx: 16 (over z, core), gy: 16 (over y, x).
Axes of the slice: x: 4, y: 4, z: 8, core: 2. Of those that a mesh axis runs over, the one named last changes fastest.
Arguments:
- basis: float32 [16, 16, 96, 2048], P('gx', 'gy')
- block_vals: float32 [16, 16, 16, 5, 128, 128], P('gx', 'gy'), as said below
- block_cols: int32 [16, 16, 16, 5], P('gx', 'gy'), may hold values from 0 to 15, as said below
- edge_rows: int32 [16, 16, 4, 256], P('gx', 'gy'), may hold values from 0 to 2047, as said below
- live_counts: int32 [16, 16], P('gx', 'gy'), may hold values from 1024 to 2048, as said below
Outputs:
- encoding: float32 [16, 16, 96, 2048], P('gx', 'gy')
Inputs may be any that keep to these rules, and one draw needn't show every extreme that they name: `live_counts`: every tile has 1024 or more live cells, and some tile is full. `block_cols`: entries name blocks of the same tile. `block_vals`: weights are nonnegative; the weight between two cells is the same in both stored blocks that hold it, and a cell has no weight to itself. `edge_rows`: every entry is a live cell of its tile.
All inputs are finite; a program needn't handle non-finite values.
Results may differ from a plain program's by a relative error of at most 0.0001.
Values sent between devices are 32-bit elements; how exact they have to be, the bound alone decides.
A program may use at most 64 MiB of HBM per device.

v0:
```python
import math

import jax
import jax.numpy as jnp
from jax import lax
from jax.experimental import pallas as pl
from jax.experimental.pallas import tpu as pltpu
from jax.sharding import PartitionSpec as P

LOWER_FRACTION = 0.125
MESH = pl.DeviceIdType.MESH
F32 = jnp.float32
BF16 = jnp.bfloat16
NN = (((1,), (0,)), ((), ()))
NT = (((1,), (1,)), ((), ()))


def dot(a, b, dims=NN):
    return lax.dot_general(a, b, dims, preferred_element_type=F32)


def split(x):
    hi = x.astype(BF16)
    lo = (x - hi.astype(F32)).astype(BF16)
    return hi, lo


def inverse_factor(gram_ref, elem_ref, out_ref, scale, rows):
    blocks = rows // 8
    lane = lax.broadcasted_iota(jnp.int32, (8, 128), 1)

    def across(col):
        return jnp.broadcast_to(col, (8, 128))

    for b in range(blocks):
        first = 8 * b
        cols = {}
        for i in range(b, blocks):
            tile = gram_ref[i]
            cols[i] = [across(tile[:, first + k : first + k + 1]) for k in range(8)]
        for k in range(8):
            elem_ref[k] = cols[b][k]
        a = {
            (i, k): across(elem_ref[k, i : i + 1, :]) for k in range(8) for i in range(k, 8)
        }
        inside = (lane >= first) & (lane < first + 8)
        reduced = []
        for k in range(8):
            row = across(gram_ref[b, k : k + 1, :])
            reduced.append(jnp.where(inside, jnp.where(lane == first + k, 1.0, 0.0), row))
        inv = []
        low = {}
        for k in range(8):
            inv.append(1.0 / a[k, k])
            for i in range(k + 1, 8):
                low[i, k] = a[i, k] * inv[k]
                for j in range(k + 1, i + 1):
                    a[i, j] = a[i, j] - low[i, k] * a[j, k]
                reduced[i] = reduced[i] - low[i, k] * reduced[k]
        for i in range(b + 1, blocks):
            u = cols[i]
            for k in range(8):
                for j in range(k + 1, 8):
                    u[j] = u[j] - low[j, k] * u[k]
            tile = jnp.where(inside, 0.0, gram_ref[i])
            for k in range(8):
                tile = tile - (u[k] * inv[k]) * reduced[k]
            gram_ref[i] = tile
        for k in range(8):
            row = jnp.where(lane <= first + k, reduced[k], 0.0) * (lax.rsqrt(a[k, k]) * scale)
            out_ref[first + k : first + k + 1, :] = row[0:1, :]


def kernel(
    size_x,
    size_y,
    live_ref,
    cols_ref,
    basis_ref,
    edges_ref,
    vals_ref,
    out_ref,
    raw,
    wts,
    pick,
    place,
    vp,
    vm,
    inp,
    y0,
    ay0,
    z,
    y2,
    acc,
    deg,
    mask,
    sbuf,
    rbuf,
    mxa,
    mxb,
    gpart,
    gr1,
    gr2,
    gfull,
    elem,
    inv,
    wsem,
    hs,
    hr,
    cs,
    cr,
):
    me_x = lax.axis_index("gx")
    me_y = lax.axis_index("gy")
    blocks, stored = cols_ref.shape[2], cols_ref.shape[3]
    block = vals_ref.shape[-1]
    vecs, cells = basis_ref.shape[2], basis_ref.shape[3]
    sides, edges = edges_ref.shape[2], edges_ref.shape[3]
    group_rows = 2 * vecs

    def peer_x(d):
        return {"gx": lax.rem(me_x + d, size_x), "gy": me_y}

    def peer_y(d):
        return {"gx": me_x, "gy": lax.rem(me_y + d, size_y)}

    barrier = pltpu.get_barrier_semaphore()
    for d in range(1, size_x):
        pl.semaphore_signal(barrier, inc=1, device_id=peer_x(d), device_id_type=MESH)
    for d in range(1, size_y):
        pl.semaphore_signal(barrier, inc=1, device_id=peer_y(d), device_id_type=MESH)

    fetches = [
        pltpu.make_async_copy(vals_ref.at[0, 0, n], raw.at[n], wsem.at[n]) for n in range(blocks)
    ]
    for f in fetches:
        f.start()

    has = [me_x > 0, me_x < size_x - 1, me_y > 0, me_y < size_y - 1]
    target = [
        {"gx": me_x - 1, "gy": me_y},
        {"gx": me_x + 1, "gy": me_y},
        {"gx": me_x, "gy": me_y - 1},
        {"gx": me_x, "gy": me_y + 1},
    ]
    facing = [1, 0, 3, 2]

    def halo(app, side):
        return pltpu.make_async_remote_copy(
            src_ref=sbuf.at[app, side],
            dst_ref=rbuf.at[app, facing[side]],
            send_sem=hs.at[app, side],
            recv_sem=hr.at[app, facing[side]],
            device_id=target[side],
            device_id_type=MESH,
        )

    for side in range(sides):

        @pl.when(jnp.logical_not(has[side]))
        def _(side=side):
            for app in range(4):
                rbuf[app, side] = jnp.zeros((vecs, edges), F32)

    lane_id = lax.broadcasted_iota(jnp.int32, (8, cells), 1)
    mask[...] = jnp.where(lane_id < live_ref[0, 0], 1.0, 0.0)
    live = mask[0:1, :]
    start = basis_ref[0, 0] * live
    y0[...] = start

    def store_parts(begin, x):
        hi, lo = split(x)
        for t in range(x.shape[1] // block):
            lanes = slice(t * block, (t + 1) * block)
            vp[begin // block + t, 0:vecs, :] = hi[:, lanes]
            vp[begin // block + t, vecs:group_rows, :] = lo[:, lanes]

    def parts_at(begin, width):
        return jnp.concatenate(
            [vp[t] for t in range(begin // block, (begin + width) // block)], axis=1
        )

    store_parts(0, start)
    wide_live = jnp.broadcast_to(live, (16, cells)).astype(BF16)
    for t in range(blocks):
        vm[t] = wide_live[:, t * block : (t + 1) * block]

    step = 128

    @pl.loop(0, cells // step)
    def _(t):
        base = pl.multiple_of(t * step, step)
        cell = lax.broadcasted_iota(jnp.int32, (step, edges), 0) + base
        for side in range(sides):
            ends = edges_ref[0, 0, side : side + 1, :]
            pick[pl.ds(base, step), side * edges : (side + 1) * edges] = jnp.where(
                cell == ends, 1.0, 0.0
            ).astype(BF16)

    def send(app, pair):
        lanes = slice(pair * 2 * edges, (pair + 1) * 2 * edges)
        got = dot(parts_at(0, cells), pick[:, lanes])
        got = got[0:vecs] + got[vecs:]
        for k in range(2):
            sbuf[app, 2 * pair + k] = got[:, k * edges : (k + 1) * edges]
        for k in range(2):

            @pl.when(has[2 * pair + k])
            def _(k=k):
                halo(app, 2 * pair + k).start()

    def multiply(app, extra):
        for n in range(blocks):
            parts = []
            for s in range(stored):
                at = cols_ref[0, 0, n, s]
                part = vp[at]
                parts.append(jnp.concatenate([part, vm[at]], axis=0) if extra else part)
            got = dot(jnp.concatenate(parts, axis=1), wts[n], NT)
            here = slice(n * block, (n + 1) * block)
            acc[:, here] = got[0:vecs, 0:block] + got[vecs:group_rows, 0:block] + got[0:vecs, block:]
            if extra:
                own = got[group_rows : group_rows + 8, 0:block] + got[group_rows : group_rows + 8, block:]
                deg[:, here] = own

    def receive(app):
        for side in range(sides):

            @pl.when(has[side])
            def _(side=side):
                pltpu.make_async_remote_copy(
                    src_ref=sbuf.at[app, side],
                    dst_ref=rbuf.at[app, side],
                    send_sem=hs.at[app, side],
                    recv_sem=hr.at[app, side],
                    device_id=target[side],
                    device_id_type=MESH,
                ).wait_recv()

        for side in range(sides):
            hi, lo = split(rbuf[app, side])
            lanes = slice(side * edges, (side + 1) * edges)
            inp[0:vecs, lanes] = hi
            inp[vecs:group_rows, lanes] = lo

    chunk = 512
    chunks = [slice(q * chunk, (q + 1) * chunk) for q in range(cells // chunk)]

    def landed(sl, rows):
        return dot(inp[0:rows, :], place[:, sl])

    def exchange(kind, buf, peer, me, size):
        def one(d):
            return pltpu.make_async_remote_copy(
                src_ref=buf.at[me],
                dst_ref=buf.at[me],
                send_sem=cs.at[kind, d],
                recv_sem=cr.at[kind, d],
                device_id=peer(d),
                device_id_type=MESH,
            )

        return [one(d) for d in range(1, size)]

    def wait_from(kind, buf, me, size, peer, d):
        src = lax.rem(me + size - d, size)
        return pltpu.make_async_remote_copy(
            src_ref=buf.at[src],
            dst_ref=buf.at[src],
            send_sem=cs.at[kind, d],
            recv_sem=cr.at[kind, d],
            device_id=peer(d),
            device_id_type=MESH,
        )

    pl.semaphore_wait(barrier, size_x + size_y - 2)
    send(0, 1)
    send(0, 0)

    lane = lax.broadcasted_iota(jnp.int32, (128, 128), 1)
    for at in range(0, sides * edges, 128):
        side, from_edge = at // edges, at % edges
        ends = edges_ref[0, 0, side : side + 1, from_edge : from_edge + 128]
        col = jnp.transpose(jnp.broadcast_to(ends.astype(F32), (8, 128)))[:, 0:1]
        wide = jnp.broadcast_to(col, (128, 128)).astype(jnp.int32)
        for t in range(0, cells, 128):
            place[at : at + 128, t : t + 128] = jnp.where(wide == lane + t, 1.0, 0.0).astype(BF16)

    for side in range(sides):
        flag = jnp.where(has[side], 1.0, 0.0).astype(F32)
        inp[group_rows : group_rows + 16, side * edges : (side + 1) * edges] = jnp.full(
            (16, edges), flag, F32
        ).astype(BF16)

    for n in range(blocks):
        fetches[n].wait()
        for s in range(stored):
            hi, lo = split(raw[n, s])
            wts[n, 0:block, s * block : (s + 1) * block] = hi
            wts[n, block : 2 * block, s * block : (s + 1) * block] = lo

    multiply(0, 16)
    receive(0)
    for sl in chunks:
        got = landed(sl, group_rows + 16)
        av = acc[:, sl] + got[0:vecs] + got[vecs:group_rows]
        d = mask[:, sl] * (deg[:, sl] + got[group_rows : group_rows + 8])
        deg[:, sl] = d
        ay0[:, sl] = av
        first = mask[0:1, sl] * (d[0:1] * y0[:, sl] - av)
        z[:, sl] = first
        store_parts(sl.start, first)
    top = jnp.max(deg[...], axis=1, keepdims=True)
    mxa[me_y] = jnp.broadcast_to(top, (8, 128))
    for c in exchange(0, mxa, peer_y, me_y, size_y):
        c.start()

    send(1, 1)
    send(1, 0)
    for d in range(1, size_y):
        wait_from(0, mxa, me_y, size_y, peer_y, d).wait_recv()
    mxb[me_x] = jnp.max(mxa[...], axis=0)
    for c in exchange(1, mxb, peer_x, me_x, size_x):
        c.start()
    multiply(1, 0)
    receive(1)
    for d in range(1, size_x):
        wait_from(1, mxb, me_x, size_x, peer_x, d).wait_recv()
    upper = 2.0 * jnp.max(mxb[...], axis=0)[0:1, :]
    lower = LOWER_FRACTION * upper
    half_width = (upper - lower) / 2.0
    centre = (upper + lower) / 2.0
    over = 1.0 / half_width
    centre = centre[0:1, 0:1]
    over = over[0:1, 0:1]
    twice = 2.0 * over
    for sl in chunks:
        got = landed(sl, group_rows)
        az = acc[:, sl] + got[0:vecs] + got[vecs:]
        y1 = (z[:, sl] - centre * y0[:, sl]) * over
        ay1 = (az - centre * ay0[:, sl]) * over
        ly1 = mask[0:1, sl] * (deg[0:1, sl] * y1 - ay1)
        second = twice * (ly1 - centre * y1) - y0[:, sl]
        z[:, sl] = y1
        y2[:, sl] = second
        store_parts(sl.start, second)

    previous, current, following = z, y2, y0
    for app in (2, 3):
        send(app, 1)
        send(app, 0)
        multiply(app, 0)
        receive(app)
        for sl in chunks:
            got = landed(sl, group_rows)
            av = acc[:, sl] + got[0:vecs] + got[vecs:]
            lap = mask[0:1, sl] * (deg[0:1, sl] * current[:, sl] - av)
            new = twice * (lap - centre * current[:, sl]) - previous[:, sl]
            following[:, sl] = new
            store_parts(sl.start, new)
        previous, current, following = current, following, previous

    both = parts_at(0, cells)
    full = dot(both, both, NT)
    gram = full[0:vecs, 0:vecs] + full[0:vecs, vecs:] + full[vecs:, 0:vecs] + full[vecs:, vecs:]
    gram = jnp.concatenate([gram, jnp.zeros((vecs, 128 - vecs), F32)], axis=1)
    owners = vecs // 8
    for p in range(owners):
        gpart[p] = gram[8 * p : 8 * p + 8, :]

    def to_owner(p):
        return pltpu.make_async_remote_copy(
            src_ref=gpart.at[p],
            dst_ref=gr1.at[me_y],
            send_sem=cs.at[2, p],
            recv_sem=cr.at[2, me_y],
            device_id={"gx": me_x, "gy": p},
            device_id_type=MESH,
        )

    def from_member(q):
        return pltpu.make_async_remote_copy(
            src_ref=gr1.at[q],
            dst_ref=gr1.at[q],
            send_sem=cs.at[2, q],
            recv_sem=cr.at[2, q],
            device_id={"gx": me_x, "gy": q},
            device_id_type=MESH,
        )

    for p in range(owners):

        @pl.when(me_y != p)
        def _(p=p):
            to_owner(p).start()

    @pl.when(me_y < owners)
    def _():
        gr1[me_y] = gpart[me_y]
        for q in range(size_y):

            @pl.when(me_y != q)
            def _(q=q):
                from_member(q).wait_recv()

        gr2[me_x] = jnp.sum(gr1[...], axis=0)
        for c in exchange(3, gr2, peer_x, me_x, size_x):
            c.start()
        for d in range(1, size_x):
            wait_from(3, gr2, me_x, size_x, peer_x, d).wait_recv()
        gfull[me_y] = jnp.sum(gr2[...], axis=0)
        for c in exchange(4, gfull, peer_y, me_y, size_y):
            c.start()

    def from_owner(p):
        return pltpu.make_async_remote_copy(
            src_ref=gfull.at[p],
            dst_ref=gfull.at[p],
            send_sem=cs.at[4, 0],
            recv_sem=cr.at[4, lax.rem(me_y + size_y - p, size_y)],
            device_id={"gx": me_x, "gy": p},
            device_id_type=MESH,
        )

    for p in range(owners):

        @pl.when(me_y != p)
        def _(p=p):
            from_owner(p).wait_recv()

    for app in range(4):
        for side in range(sides):

            @pl.when(has[side])
            def _(app=app, side=side):
                halo(app, side).wait_send()

    for c in exchange(0, mxa, peer_y, me_y, size_y) + exchange(1, mxb, peer_x, me_x, size_x):
        c.wait_send()
    for p in range(owners):

        @pl.when(me_y != p)
        def _(p=p):
            to_owner(p).wait_send()

    @pl.when(me_y < owners)
    def _():
        for c in exchange(3, gr2, peer_x, me_x, size_x) + exchange(4, gfull, peer_y, me_y, size_y):
            c.wait_send()

    total = cells * size_x * size_y
    inverse_factor(gfull, elem, inv, math.sqrt(total), vecs)
    hi, lo = split(inv[...])
    hi, lo = hi[:, 0:vecs], lo[:, 0:vecs]
    left = jnp.concatenate(
        [jnp.concatenate([hi, hi], axis=1), jnp.concatenate([lo, lo], axis=1)], axis=0
    )
    for sl in chunks:
        got = dot(left, parts_at(sl.start, chunk))
        out_ref[0, 0, :, sl] = got[0:vecs] + got[vecs:]


def per_device(size_x, size_y, basis, block_vals, block_cols, edge_rows, live_counts):
    blocks, stored, block = block_vals.shape[2:5]
    vecs, cells = basis.shape[2:]
    sides, edges = edge_rows.shape[2:]
    vmem = pltpu.VMEM
    field = vmem((vecs, cells), F32)
    scratch = [
        vmem((blocks, stored, block, block), F32),
        vmem((blocks, 2 * block, stored * block), BF16),
        vmem((cells, sides * edges), BF16),
        vmem((sides * edges, cells), BF16),
        vmem((blocks, 2 * vecs, block), BF16),
        vmem((blocks, 16, block), BF16),
        vmem((2 * vecs + 16, sides * edges), BF16),
        field,
        field,
        field,
        field,
        field,
        vmem((8, cells), F32),
        vmem((8, cells), F32),
        vmem((4, sides, vecs, edges), F32),
        vmem((4, sides, vecs, edges), F32),
        vmem((size_y, 8, 128), F32),
        vmem((size_x, 8, 128), F32),
        vmem((vecs // 8, 8, 128), F32),
        vmem((size_y, 8, 128), F32),
        vmem((size_x, 8, 128), F32),
        vmem((vecs // 8, 8, 128), F32),
        vmem((8, 8, 128), F32),
        vmem((vecs, 128), F32),
        pltpu.SemaphoreType.DMA((blocks,)),
        pltpu.SemaphoreType.DMA((4, sides)),
        pltpu.SemaphoreType.DMA((4, sides)),
        pltpu.SemaphoreType.DMA((5, max(size_x, size_y))),
        pltpu.SemaphoreType.DMA((5, max(size_x, size_y))),
    ]
    in_vmem = pl.BlockSpec(memory_space=vmem)
    in_smem = pl.BlockSpec(memory_space=pltpu.SMEM)
    return pl.pallas_call(
        lambda *refs: kernel(size_x, size_y, *refs),
        out_shape=jax.ShapeDtypeStruct(basis.shape, F32),
        in_specs=[in_smem, in_smem, in_vmem, in_vmem, pl.BlockSpec(memory_space=pl.ANY)],
        out_specs=in_vmem,
        scratch_shapes=scratch,
        compiler_params=pltpu.CompilerParams(
            collective_id=0, has_side_effects=True, vmem_limit_bytes=56 * 2**20
        ),
        name="filtered_subspace_step",
    )(live_counts, block_cols, basis, edge_rows, block_vals)


def solution(mesh):
    size_x, size_y = mesh.shape["gx"], mesh.shape["gy"]
    in_specs = (
        P("gx", "gy", None, None),
        P("gx", "gy", None, None, None, None),
        P("gx", "gy", None, None),
        P("gx", "gy", None, None),
        P("gx", "gy"),
    )
    out_specs = P("gx", "gy", None, None)
    return jax.shard_map(
        lambda *args: per_device(size_x, size_y, *args),
        mesh=mesh,
        in_specs=in_specs,
        out_specs=out_specs,
        check_vma=False,
    )
```

profile of v0, /device:TPU:1, one launch (start us, length us, event | category | flops | bytes accessed | tf_op | source)
XLA Modules:
  0.0 66.1 jit_solution(61631934587620598)
XLA Ops:
  0.7 1.4 %copy.6.refs_1_ = s32[1,1,16,5]{3,2,1,0:T(8,128)} copy(s32[1,1,16,5]{2,1,3,0:T(1,128)} %param.7) | data formatting | bytes 640 | tf_op args[2]
  2.0 62.0 %filtered_subspace_step.1 = f32[1,1,96,2048]{3,2,1,0:T(8,128)} custom-call(s32[1,1]{1,0:T(1,128)S(6)} %copy.8.refs_0_, s32[1,1,16,5]{3,2,1,0:T(8,128)} %copy.6.refs_1_, f32[1,1,96,2048]{3,2,1,0:T(8,128)} %refs_2_.1, s32[1,1,4,256]{3,2,1,0:T(4,128)} %refs_3_.1, f32[1,1,16,5,128,128]{5,4,3,2,1,0:T(8,128)} %refs_4_.1), custom_call_target="tpu_custom_call" | custom-call | tf_op jit(solution)/shard_map/filtered_subspace_step/pallas_call | solution.py:502
  64.0 2.1 %copy.9 = f32[1,1,96,2048]{3,2,1,0:T(8,128)} copy(f32[1,1,96,2048]{3,2,1,0:T(8,128)} %filtered_subspace_step.1) | data formatting | bytes 1572864
where the time goes:
time: 66.2 us; the launch traced here: 66.1 us
  Pallas kernels  62 us (94%)
  local copies, waits for them, and re-layouts  3.42 us (5%)
    pallas_call x1, Pallas kernels, per_device(): pl.pallas_call(lambda *refs: kernel(size_x, size_y, *refs), out_shape=jax...  62 us
    unnamed x2, local copies, waits for them, and re-layouts  3.42 us

commit v1 on v0

v1 whole, which is shorter than its diff:
```python
import math

import jax
import jax.numpy as jnp
from jax import lax
from jax.experimental import pallas as pl
from jax.experimental.pallas import tpu as pltpu
from jax.sharding import PartitionSpec as P

LOWER_FRACTION = 0.125
MESH = pl.DeviceIdType.MESH
F32 = jnp.float32
BF16 = jnp.bfloat16
NN = (((1,), (0,)), ((), ()))
NT = (((1,), (1,)), ((), ()))


def dot(a, b, dims=NN):
    return lax.dot_general(a, b, dims, preferred_element_type=F32)


def split(x):
    hi = x.astype(BF16)
    lo = (x - hi.astype(F32)).astype(BF16)
    return hi, lo


def inverse_factor(gram_ref, elem_ref, out_ref, scale, rows):
    blocks = rows // 8
    lane = lax.broadcasted_iota(jnp.int32, (8, 128), 1)

    def across(col):
        return jnp.broadcast_to(col, (8, 128))

    for b in range(blocks):
        first = 8 * b
        cols = {}
        for i in range(b, blocks):
            tile = gram_ref[i]
            cols[i] = [across(tile[:, first + k : first + k + 1]) for k in range(8)]
        for k in range(8):
            elem_ref[k] = cols[b][k]
        a = {
            (i, k): across(elem_ref[k, i : i + 1, :]) for k in range(8) for i in range(k, 8)
        }
        inside = (lane >= first) & (lane < first + 8)
        reduced = []
        for k in range(8):
            row = across(gram_ref[b, k : k + 1, :])
            reduced.append(jnp.where(inside, jnp.where(lane == first + k, 1.0, 0.0), row))
        inv = []
        low = {}
        for k in range(8):
            inv.append(1.0 / a[k, k])
            for i in range(k + 1, 8):
                low[i, k] = a[i, k] * inv[k]
                for j in range(k + 1, i + 1):
                    a[i, j] = a[i, j] - low[i, k] * a[j, k]
                reduced[i] = reduced[i] - low[i, k] * reduced[k]
        for i in range(b + 1, blocks):
            u = cols[i]
            for k in range(8):
                for j in range(k + 1, 8):
                    u[j] = u[j] - low[j, k] * u[k]
            tile = jnp.where(inside, 0.0, gram_ref[i])
            for k in range(8):
                tile = tile - (u[k] * inv[k]) * reduced[k]
            gram_ref[i] = tile
        for k in range(8):
            row = jnp.where(lane <= first + k, reduced[k], 0.0) * (lax.rsqrt(a[k, k]) * scale)
            out_ref[first + k : first + k + 1, :] = row[0:1, :]


def filter_kernel(
    size_x,
    size_y,
    live_ref,
    cols_ref,
    basis_ref,
    edges_ref,
    vals_ref,
    vp,
    gfull,
    raw,
    wts,
    pick,
    place,
    same,
    vm,
    inp,
    fa,
    fb,
    rest,
    deg,
    mask,
    sbuf,
    rbuf,
    mxa,
    mxb,
    gpart,
    gr1,
    gr2,
    wsem,
    hs,
    hr,
    cs,
    cr,
):
    me_x = lax.axis_index("gx")
    me_y = lax.axis_index("gy")
    stored, blocks = cols_ref.shape[1], cols_ref.shape[3]
    block = vals_ref.shape[-1]
    vecs, cells = basis_ref.shape[2], basis_ref.shape[3]
    sides, edges = edges_ref.shape[2], edges_ref.shape[3]
    ends_all = sides * edges
    group_rows = 2 * vecs

    def peer_x(d):
        return {"gx": lax.rem(me_x + d, size_x), "gy": me_y}

    def peer_y(d):
        return {"gx": me_x, "gy": lax.rem(me_y + d, size_y)}

    barrier = pltpu.get_barrier_semaphore()
    for d in range(1, size_x):
        pl.semaphore_signal(barrier, inc=1, device_id=peer_x(d), device_id_type=MESH)
    for d in range(1, size_y):
        pl.semaphore_signal(barrier, inc=1, device_id=peer_y(d), device_id_type=MESH)

    fetches = [
        pltpu.make_async_copy(vals_ref.at[0, 0, n], raw.at[n], wsem.at[n]) for n in range(blocks)
    ]
    for f in fetches:
        f.start()

    has = [me_x > 0, me_x < size_x - 1, me_y > 0, me_y < size_y - 1]
    target = [
        {"gx": me_x - 1, "gy": me_y},
        {"gx": me_x + 1, "gy": me_y},
        {"gx": me_x, "gy": me_y - 1},
        {"gx": me_x, "gy": me_y + 1},
    ]
    facing = [1, 0, 3, 2]
    scaled = 1

    def halo(app, side, into):
        rows = vecs + 8 if app == scaled else vecs
        return pltpu.make_async_remote_copy(
            src_ref=sbuf.at[app, side, pl.ds(0, rows)],
            dst_ref=rbuf.at[app, into, pl.ds(0, rows)],
            send_sem=hs.at[app, side],
            recv_sem=hr.at[app, into],
            device_id=target[side],
            device_id_type=MESH,
        )

    for side in range(sides):

        @pl.when(jnp.logical_not(has[side]))
        def _(side=side):
            for app in range(4):
                rbuf[app, side] = jnp.zeros((vecs + 8, edges), F32)

    lane_id = lax.broadcasted_iota(jnp.int32, (8, cells), 1)
    mask[...] = jnp.where(lane_id < live_ref[0, 0], 1.0, 0.0)

    def store_parts(begin, x):
        hi, lo = split(x)
        for t in range(x.shape[1] // block):
            lanes = slice(t * block, (t + 1) * block)
            vp[begin // block + t, 0:vecs, :] = hi[:, lanes]
            vp[begin // block + t, vecs:group_rows, :] = lo[:, lanes]

    def parts_at(begin, width):
        return jnp.concatenate(
            [vp[t] for t in range(begin // block, (begin + width) // block)], axis=1
        )

    start = basis_ref[0, 0] * mask[0:1, :]
    fa[...] = start
    store_parts(0, start)

    step = 128

    @pl.loop(0, cells // step)
    def _(t):
        base = pl.multiple_of(t * step, step)
        cell = lax.broadcasted_iota(jnp.int32, (step, edges), 0) + base
        for side in range(sides):
            ends = edges_ref[0, 0, side : side + 1, :]
            pick[pl.ds(base, step), side * edges : (side + 1) * edges] = jnp.where(
                cell == ends, 1.0, 0.0
            ).astype(BF16)

    chunk = 512
    chunks = [slice(q * chunk, (q + 1) * chunk) for q in range(cells // chunk)]
    pair = 2 * edges

    def gather(k):
        got = dot(parts_at(0, cells), pick[:, k * pair : (k + 1) * pair])
        return got[0:vecs] + got[vecs:]

    def send(app, k, values):
        for i in range(2):
            sbuf[app, 2 * k + i, 0:vecs, :] = values[:, i * edges : (i + 1) * edges]
        for i in range(2):

            @pl.when(has[2 * k + i])
            def _(i=i):
                halo(app, 2 * k + i, facing[2 * k + i]).start()

    def sent(app, k):
        return jnp.concatenate([sbuf[app, 2 * k, 0:vecs, :], sbuf[app, 2 * k + 1, 0:vecs, :]], axis=1)

    def multiply(use, width):
        for n in range(blocks):
            got = dot(
                jnp.concatenate([vp[cols_ref[0, s, 0, n]] for s in range(stored)], axis=1),
                wts[n],
                NT,
            )
            use(
                slice(n * block, (n + 1) * block),
                got[0:vecs, 0:width] + got[vecs:, 0:width] + got[0:vecs, width:],
            )

    def receive(app, factor):
        for side in range(sides):

            @pl.when(has[side])
            def _(side=side):
                halo(app, side, side).wait_recv()

        for side in range(sides):
            came = rbuf[app, side, 0:vecs, :]
            if factor is not None:
                came = came * (rbuf[app, side, vecs : vecs + 1, 0:1] * factor)
            hi, lo = split(came)
            lanes = slice(side * edges, (side + 1) * edges)
            inp[0:vecs, lanes] = hi
            inp[vecs:group_rows, lanes] = lo

    def across(k):
        got = dot(inp[...], same[:, k * pair : (k + 1) * pair])
        return got[0:vecs] + got[vecs:]

    def landed(sl):
        got = dot(inp[...], place[:, sl])
        return got[0:vecs] + got[vecs:]

    def exchange(kind, buf, peer, me, size):
        def one(d):
            return pltpu.make_async_remote_copy(
                src_ref=buf.at[me],
                dst_ref=buf.at[me],
                send_sem=cs.at[kind, d],
                recv_sem=cr.at[kind, d],
                device_id=peer(d),
                device_id_type=MESH,
            )

        return [one(d) for d in range(1, size)]

    def wait_from(kind, buf, me, size, peer, d):
        src = lax.rem(me + size - d, size)
        return pltpu.make_async_remote_copy(
            src_ref=buf.at[src],
            dst_ref=buf.at[src],
            send_sem=cs.at[kind, d],
            recv_sem=cr.at[kind, d],
            device_id=peer(d),
            device_id_type=MESH,
        )

    first = [gather(1), gather(0)]
    pl.semaphore_wait(barrier, size_x + size_y - 2)
    send(0, 1, first[0])
    send(0, 0, first[1])

    for n in range(blocks):
        fetches[n].wait()
        for s in range(stored):
            hi, lo = split(raw[n, s])
            wts[n, 0:block, s * block : (s + 1) * block] = hi
            wts[n, block : 2 * block, s * block : (s + 1) * block] = lo
    wide_live = jnp.broadcast_to(mask[0:1, :], (16, cells)).astype(BF16)
    for t in range(blocks):
        vm[t] = wide_live[:, t * block : (t + 1) * block]
    flags = jnp.concatenate(
        [jnp.full((16, edges), jnp.where(h, 1.0, 0.0).astype(F32), F32) for h in has], axis=1
    ).astype(BF16)
    for sl in chunks:
        deg[:, sl] = dot(flags, pick[sl, :], NT)[0:8]
    for n in range(blocks):
        here = slice(n * block, (n + 1) * block)
        got = dot(
            jnp.concatenate([vm[cols_ref[0, s, 0, n]] for s in range(stored)], axis=1), wts[n], NT
        )
        own = got[0:8, 0:block] + got[0:8, block:]
        deg[:, here] = mask[:, here] * (deg[:, here] + own)
    top = jnp.max(deg[...], axis=1, keepdims=True)
    mxa[me_y] = jnp.broadcast_to(top, (8, 128))
    for c in exchange(0, mxa, peer_y, me_y, size_y):
        c.start()
    local = 2.0 * top[0:1, :]
    local = jnp.where(local > 0.0, local, 1.0)
    shrink = 1.0 / local
    for side in range(sides):
        sbuf[scaled, side, vecs : vecs + 8, :] = jnp.broadcast_to(local, (8, edges))

    def local_z(here, wv):
        rest[:, here] = mask[0:1, here] * (deg[0:1, here] * fa[:, here] - wv) * shrink

    multiply(local_z, block)

    lane = lax.broadcasted_iota(jnp.int32, (128, 128), 1)
    for at in range(0, ends_all, 128):
        side, from_edge = at // edges, at % edges
        ends = edges_ref[0, 0, side : side + 1, from_edge : from_edge + 128]
        col = jnp.transpose(jnp.broadcast_to(ends.astype(F32), (8, 128)))[:, 0:1]
        wide = jnp.broadcast_to(col, (128, 128)).astype(jnp.int32)
        for t in range(0, cells, 128):
            place[at : at + 128, t : t + 128] = jnp.where(wide == lane + t, 1.0, 0.0).astype(BF16)
        for t in range(0, ends_all, 128):
            other = edges_ref[0, 0, t // edges : t // edges + 1, t % edges : t % edges + 128]
            same[at : at + 128, t : t + 128] = jnp.where(wide == other, 1.0, 0.0).astype(BF16)

    for sl in chunks:
        store_parts(sl.start, rest[:, sl])
    ahead = [gather(0), gather(1)]
    receive(0, None)
    for k in (1, 0):
        send(1, k, ahead[k] - across(k) * shrink)
    for sl in chunks:
        z = rest[:, sl] - mask[0:1, sl] * landed(sl) * shrink
        fb[:, sl] = z
        store_parts(sl.start, z)

    for d in range(1, size_y):
        wait_from(0, mxa, me_y, size_y, peer_y, d).wait_recv()
    mxb[me_x] = jnp.max(mxa[...], axis=0)
    for c in exchange(1, mxb, peer_x, me_x, size_x):
        c.start()

    def local_lz(here, wv):
        rest[:, here] = mask[0:1, here] * (deg[0:1, here] * fb[:, here] - wv)

    multiply(local_lz, block)
    for sl in chunks:
        store_parts(sl.start, rest[:, sl])
    ahead = [gather(0), gather(1)]
    receive(1, shrink)
    for d in range(1, size_x):
        wait_from(1, mxb, me_x, size_x, peer_x, d).wait_recv()
    upper = 2.0 * jnp.max(mxb[...], axis=0)[0:1, 0:1]
    lower = LOWER_FRACTION * upper
    half_width = (upper - lower) / 2.0
    centre = (upper + lower) / 2.0
    over = 1.0 / half_width
    ratio = centre * over
    grow = local * over

    def y2_of(lz, z, y0):
        return 2.0 * (grow * (lz * over) - (2.0 * ratio * grow) * z + (ratio * ratio) * y0) - y0

    for k in (1, 0):
        send(2, k, y2_of(ahead[k] - across(k), sent(1, k), sent(0, k)))
    for sl in chunks:
        lz = rest[:, sl] - mask[0:1, sl] * landed(sl)
        z, y0 = fb[:, sl], fa[:, sl]
        y2 = y2_of(lz, z, y0)
        fb[:, sl] = y2
        fa[:, sl] = grow * z - ratio * y0
        store_parts(sl.start, y2)

    twice = 2.0 * over
    previous, current = fa, fb
    for app in (2, 3):

        def local_next(here, wv, previous=previous, current=current):
            y = current[:, here]
            lap = mask[0:1, here] * (deg[0:1, here] * y - wv)
            rest[:, here] = twice * (lap - centre * y) - previous[:, here]

        multiply(local_next, block)
        if app == 2:
            for sl in chunks:
                store_parts(sl.start, rest[:, sl])
            ahead = [gather(0), gather(1)]
        receive(app, None)
        if app == 2:
            for k in (1, 0):
                send(3, k, ahead[k] - twice * across(k))
        for sl in chunks:
            new = rest[:, sl] - mask[0:1, sl] * (twice * landed(sl))
            if app == 2:
                previous[:, sl] = new
            store_parts(sl.start, new)
        previous, current = current, previous

    both = parts_at(0, cells)
    full = dot(both, both, NT)
    gram = full[0:vecs, 0:vecs] + full[0:vecs, vecs:] + full[vecs:, 0:vecs] + full[vecs:, vecs:]
    gram = jnp.concatenate([gram, jnp.zeros((vecs, 128 - vecs), F32)], axis=1)
    owners = vecs // 8
    for p in range(owners):
        gpart[p] = gram[8 * p : 8 * p + 8, :]

    def to_owner(p):
        return pltpu.make_async_remote_copy(
            src_ref=gpart.at[p],
            dst_ref=gr1.at[me_y],
            send_sem=cs.at[2, p],
            recv_sem=cr.at[2, me_y],
            device_id={"gx": me_x, "gy": p},
            device_id_type=MESH,
        )

    def from_member(q):
        return pltpu.make_async_remote_copy(
            src_ref=gr1.at[q],
            dst_ref=gr1.at[q],
            send_sem=cs.at[2, q],
            recv_sem=cr.at[2, q],
            device_id={"gx": me_x, "gy": q},
            device_id_type=MESH,
        )

    def from_owner(p):
        return pltpu.make_async_remote_copy(
            src_ref=gfull.at[p],
            dst_ref=gfull.at[p],
            send_sem=cs.at[4, 0],
            recv_sem=cr.at[4, lax.rem(me_y + size_y - p, size_y)],
            device_id={"gx": me_x, "gy": p},
            device_id_type=MESH,
        )

    for p in range(owners):

        @pl.when(me_y != p)
        def _(p=p):
            to_owner(p).start()

    @pl.when(me_y < owners)
    def _():
        gr1[me_y] = gpart[me_y]
        for q in range(size_y):

            @pl.when(me_y != q)
            def _(q=q):
                from_member(q).wait_recv()

        gr2[me_x] = jnp.sum(gr1[...], axis=0)
        for c in exchange(3, gr2, peer_x, me_x, size_x):
            c.start()
        for d in range(1, size_x):
            wait_from(3, gr2, me_x, size_x, peer_x, d).wait_recv()
        gfull[me_y] = jnp.sum(gr2[...], axis=0)
        for c in exchange(4, gfull, peer_y, me_y, size_y):
            c.start()

    for app in range(4):
        for side in range(sides):

            @pl.when(has[side])
            def _(app=app, side=side):
                halo(app, side, facing[side]).wait_send()

    for c in exchange(0, mxa, peer_y, me_y, size_y) + exchange(1, mxb, peer_x, me_x, size_x):
        c.wait_send()
    for p in range(owners):

        @pl.when(me_y != p)
        def _(p=p):
            to_owner(p).wait_send()

    for p in range(owners):

        @pl.when(me_y != p)
        def _(p=p):
            from_owner(p).wait_recv()

    @pl.when(me_y < owners)
    def _():
        for c in exchange(3, gr2, peer_x, me_x, size_x) + exchange(4, gfull, peer_y, me_y, size_y):
            c.wait_send()


def finish_kernel(scale, gram_ref, parts_ref, out_ref, work, elem, inv):
    vecs = out_ref.shape[2]

    @pl.when(pl.program_id(0) == 0)
    def _():
        work[...] = gram_ref[...]
        inverse_factor(work, elem, inv, scale, vecs)

    hi, lo = split(inv[...])
    hi, lo = hi[:, 0:vecs], lo[:, 0:vecs]
    left = jnp.concatenate(
        [jnp.concatenate([hi, hi], axis=1), jnp.concatenate([lo, lo], axis=1)], axis=0
    )
    right = jnp.concatenate([parts_ref[t] for t in range(parts_ref.shape[0])], axis=1)
    got = dot(left, right)
    out_ref[0, 0] = got[0:vecs] + got[vecs:]


def per_device(size_x, size_y, basis, block_vals, block_cols, edge_rows, live_counts):
    blocks, stored, block = block_vals.shape[2:5]
    vecs, cells = basis.shape[2:]
    sides, edges = edge_rows.shape[2:]
    ends = sides * edges
    vmem = pltpu.VMEM
    field = vmem((vecs, cells), F32)
    scratch = [
        vmem((blocks, stored, block, block), F32),
        vmem((blocks, 2 * block, stored * block), BF16),
        vmem((cells, ends), BF16),
        vmem((ends, cells), BF16),
        vmem((ends, ends), BF16),
        vmem((blocks, 16, block), BF16),
        vmem((2 * vecs, ends), BF16),
        field,
        field,
        field,
        vmem((8, cells), F32),
        vmem((8, cells), F32),
        vmem((4, sides, vecs + 8, edges), F32),
        vmem((4, sides, vecs + 8, edges), F32),
        vmem((size_y, 8, 128), F32),
        vmem((size_x, 8, 128), F32),
        vmem((vecs // 8, 8, 128), F32),
        vmem((size_y, 8, 128), F32),
        vmem((size_x, 8, 128), F32),
        pltpu.SemaphoreType.DMA((blocks,)),
        pltpu.SemaphoreType.DMA((4, sides)),
        pltpu.SemaphoreType.DMA((4, sides)),
        pltpu.SemaphoreType.DMA((5, max(size_x, size_y))),
        pltpu.SemaphoreType.DMA((5, max(size_x, size_y))),
    ]
    in_vmem = pl.BlockSpec(memory_space=vmem)
    in_smem = pl.BlockSpec(memory_space=pltpu.SMEM)
    parts, gram = pl.pallas_call(
        lambda *refs: filter_kernel(size_x, size_y, *refs),
        out_shape=[
            jax.ShapeDtypeStruct((blocks, 2 * vecs, block), BF16),
            jax.ShapeDtypeStruct((vecs // 8, 8, 128), F32),
        ],
        in_specs=[in_smem, in_smem, in_vmem, in_vmem, pl.BlockSpec(memory_space=pl.ANY)],
        out_specs=[in_vmem, in_vmem],
        scratch_shapes=scratch,
        compiler_params=pltpu.CompilerParams(
            collective_id=0, has_side_effects=True, vmem_limit_bytes=60 * 2**20
        ),
        name="filter_and_gram",
    )(live_counts, jnp.transpose(block_cols, (0, 3, 1, 2)), basis, edge_rows, block_vals)
    steps = 4
    return pl.pallas_call(
        lambda *refs: finish_kernel(math.sqrt(cells * size_x * size_y), *refs),
        out_shape=jax.ShapeDtypeStruct(basis.shape, F32),
        grid=(steps,),
        in_specs=[
            pl.BlockSpec(gram.shape, lambda i: (0, 0, 0)),
            pl.BlockSpec((blocks // steps, 2 * vecs, block), lambda i: (i, 0, 0)),
        ],
        out_specs=pl.BlockSpec((1, 1, vecs, cells // steps), lambda i: (0, 0, 0, i)),
        scratch_shapes=[
            vmem(gram.shape, F32),
            vmem((8, 8, 128), F32),
            vmem((vecs, 128), F32),
        ],
        compiler_params=pltpu.CompilerParams(vmem_limit_bytes=60 * 2**20),
        name="factor_and_encode",
    )(gram, parts)


def solution(mesh):
    size_x, size_y = mesh.shape["gx"], mesh.shape["gy"]
    in_specs = (
        P("gx", "gy", None, None),
        P("gx", "gy", None, None, None, None),
        P("gx", "gy", None, None),
        P("gx", "gy", None, None),
        P("gx", "gy"),
    )
    out_specs = P("gx", "gy", None, None)
    return jax.shard_map(
        lambda *args: per_device(size_x, size_y, *args),
        mesh=mesh,
        in_specs=in_specs,
        out_specs=out_specs,
        check_vma=False,
    )
```

time: 66.2 us -> 62.4 us (0.943)
  local copies, waits for them, and re-layouts: 3.42 us -> 0 us
    unnamed x2 -> x0, local copies, waits for them, and re-layouts: 3.42 us -> none
    pallas_call x1 -> x2, Pallas kernels: 62 us -> 61.6 us  [the longest x1 55.2 us: per_device(): pl.pallas_call(lambda *refs: filter_kernel(size_x, size_y, *refs), out_sh...]
where the time goes in v1:
time: 62.4 us; the launch traced here: 62.2 us
  Pallas kernels  61.6 us (99%)
  between operations  0.66 us (1%)
    pallas_call x1, Pallas kernels, per_device(): pl.pallas_call(lambda *refs: filter_kernel(size_x, size_y, *refs), out_sh...  55.2 us
    pallas_call x1, Pallas kernels, per_device(): pl.pallas_call(lambda *refs: finish_kernel(math.sqrt(cells * size_x * siz...  6.37 us

profile of v1, /device:TPU:1, one launch (start us, length us, event | category | flops | bytes accessed | tf_op | source)
XLA Modules:
  0.0 62.2 jit_solution(7420799473532269267)
XLA Ops:
  0.7 55.2 %filter_and_gram.1 = (bf16[16,192,128]{2,1,0:T(8,128)(2,1)}, f32[12,8,128]{2,1,0:T(8,128)}) custom-call(s32[1,1]{1,0:T(1,128)S(6)} %copy.6.refs_0_, s32[1,5,1,16]{3,2,1,0:T(1,128)} %bitcast.1, f32[1,1,96,2048]{3,2,1,0:T(8,128)} %refs_2_.1, s32[1,1,4,256]{3,2,1,0:T(4,128)} %refs_3_.1, f32[1,1,16,5,128,128]{5,4,3,2,1,0:T(8,128)} %refs_4_.1), custom_call_target="tpu_custom_call" | custom-call | tf_op jit(solution)/shard_map/filter_and_gram/pallas_call | solution.py:543
  55.9 6.4 %factor_and_encode.1 = f32[1,1,96,2048]{3,2,1,0:T(8,128)} custom-call(f32[12,8,128]{2,1,0:T(8,128)} %get-tuple-element.7.refs_0_, bf16[16,192,128]{2,1,0:T(8,128)(2,1)} %get-tuple-element.8.refs_1_), custom_call_target="tpu_custom_call" | custom-call | tf_op jit(solution)/shard_map/factor_and_encode/pallas_call | solution.py:558

commit v2 on v1

--- a/solution.py
+++ b/solution.py
@@ -71,6 +71,10 @@
             out_ref[first + k : first + k + 1, :] = row[0:1, :]
 
 
+def far_first(size):
+    return sorted(range(1, size), key=lambda d: -min(d, size - d))
+
+
 def filter_kernel(
     size_x,
     size_y,
@@ -79,8 +83,10 @@
     basis_ref,
     edges_ref,
     vals_ref,
+    parts_ref,
+    gfull,
     vp,
-    gfull,
+    rp,
     raw,
     wts,
     pick,
@@ -101,6 +107,7 @@
     gr1,
     gr2,
     wsem,
+    psem,
     hs,
     hr,
     cs,
@@ -164,17 +171,15 @@
     lane_id = lax.broadcasted_iota(jnp.int32, (8, cells), 1)
     mask[...] = jnp.where(lane_id < live_ref[0, 0], 1.0, 0.0)
 
-    def store_parts(begin, x):
+    def store_parts(begin, x, into=vp):
         hi, lo = split(x)
         for t in range(x.shape[1] // block):
             lanes = slice(t * block, (t + 1) * block)
-            vp[begin // block + t, 0:vecs, :] = hi[:, lanes]
-            vp[begin // block + t, vecs:group_rows, :] = lo[:, lanes]
-
-    def parts_at(begin, width):
-        return jnp.concatenate(
-            [vp[t] for t in range(begin // block, (begin + width) // block)], axis=1
-        )
+            into[begin // block + t, 0:vecs, :] = hi[:, lanes]
+            into[begin // block + t, vecs:group_rows, :] = lo[:, lanes]
+
+    def all_parts(src):
+        return jnp.concatenate([src[t] for t in range(blocks)], axis=1)
 
     start = basis_ref[0, 0] * mask[0:1, :]
     fa[...] = start
@@ -196,8 +201,8 @@
     chunks = [slice(q * chunk, (q + 1) * chunk) for q in range(cells // chunk)]
     pair = 2 * edges
 
-    def gather(k):
-        got = dot(parts_at(0, cells), pick[:, k * pair : (k + 1) * pair])
+    def gather(k, src):
+        got = dot(all_parts(src), pick[:, k * pair : (k + 1) * pair])
         return got[0:vecs] + got[vecs:]
 
     def send(app, k, values):
@@ -259,7 +264,7 @@
                 device_id_type=MESH,
             )
 
-        return [one(d) for d in range(1, size)]
+        return [one(d) for d in far_first(size)]
 
     def wait_from(kind, buf, me, size, peer, d):
         src = lax.rem(me + size - d, size)
@@ -272,30 +277,46 @@
             device_id_type=MESH,
         )
 
-    first = [gather(1), gather(0)]
+    ahead = gather(1, vp)
     pl.semaphore_wait(barrier, size_x + size_y - 2)
-    send(0, 1, first[0])
-    send(0, 0, first[1])
-
+    send(0, 1, ahead)
+    send(0, 0, gather(0, vp))
+
+    lane = lax.broadcasted_iota(jnp.int32, (128, 128), 1)
+
+    def down(at):
+        side, from_edge = at // edges, at % edges
+        ends = edges_ref[0, 0, side : side + 1, from_edge : from_edge + 128]
+        col = jnp.transpose(jnp.broadcast_to(ends.astype(F32), (8, 128)))[:, 0:1]
+        return jnp.broadcast_to(col, (128, 128)).astype(jnp.int32)
+
+    counts = [jnp.zeros((8, 128), F32) for _ in range(cells // 128)]
+    for at in range(0, ends_all, 128):
+        wide = down(at)
+        flag = jnp.where(has[at // edges], 1.0, 0.0).astype(F32)
+        for t in range(cells // 128):
+            hit = jnp.where(wide == lane + t * 128, 1.0, 0.0)
+            place[at : at + 128, t * 128 : (t + 1) * 128] = hit.astype(BF16)
+            counts[t] = counts[t] + flag * jnp.sum(hit.reshape(16, 8, 128), axis=0)
+    for t in range(cells // 128):
+        deg[:, t * 128 : (t + 1) * 128] = jnp.broadcast_to(
+            jnp.sum(counts[t], axis=0, keepdims=True), (8, 128)
+        )
+
+    for t in range(blocks):
+        vm[t] = mask[:, t * block : (t + 1) * block]
+    ones = jnp.ones((16, block), BF16)
     for n in range(blocks):
         fetches[n].wait()
+        heavy = jnp.zeros((block, block), F32)
         for s in range(stored):
-            hi, lo = split(raw[n, s])
+            w = raw[n, s]
+            hi, lo = split(w)
             wts[n, 0:block, s * block : (s + 1) * block] = hi
             wts[n, block : 2 * block, s * block : (s + 1) * block] = lo
-    wide_live = jnp.broadcast_to(mask[0:1, :], (16, cells)).astype(BF16)
-    for t in range(blocks):
-        vm[t] = wide_live[:, t * block : (t + 1) * block]
-    flags = jnp.concatenate(
-        [jnp.full((16, edges), jnp.where(h, 1.0, 0.0).astype(F32), F32) for h in has], axis=1
-    ).astype(BF16)
-    for sl in chunks:
-        deg[:, sl] = dot(flags, pick[sl, :], NT)[0:8]
-    for n in range(blocks):
+            heavy = heavy + w * vm[cols_ref[0, s, 0, n]][0:1, :]
         here = slice(n * block, (n + 1) * block)
-        got = dot(
-            jnp.concatenate([vm[cols_ref[0, s, 0, n]] for s in range(stored)], axis=1), wts[n], NT
-        )
+        got = dot(ones, jnp.concatenate(split(heavy), axis=0), NT)
         own = got[0:8, 0:block] + got[0:8, block:]
         deg[:, here] = mask[:, here] * (deg[:, here] + own)
     top = jnp.max(deg[...], axis=1, keepdims=True)
@@ -308,47 +329,41 @@
     for side in range(sides):
         sbuf[scaled, side, vecs : vecs + 8, :] = jnp.broadcast_to(local, (8, edges))
 
+    def keep(here, x, for_edges=True):
+        rest[:, here] = x
+        if for_edges:
+            store_parts(here.start, x, rp)
+
     def local_z(here, wv):
-        rest[:, here] = mask[0:1, here] * (deg[0:1, here] * fa[:, here] - wv) * shrink
+        keep(here, mask[0:1, here] * (deg[0:1, here] * fa[:, here] - wv) * shrink)
 
     multiply(local_z, block)
 
-    lane = lax.broadcasted_iota(jnp.int32, (128, 128), 1)
     for at in range(0, ends_all, 128):
-        side, from_edge = at // edges, at % edges
-        ends = edges_ref[0, 0, side : side + 1, from_edge : from_edge + 128]
-        col = jnp.transpose(jnp.broadcast_to(ends.astype(F32), (8, 128)))[:, 0:1]
-        wide = jnp.broadcast_to(col, (128, 128)).astype(jnp.int32)
-        for t in range(0, cells, 128):
-            place[at : at + 128, t : t + 128] = jnp.where(wide == lane + t, 1.0, 0.0).astype(BF16)
+        wide = down(at)
         for t in range(0, ends_all, 128):
             other = edges_ref[0, 0, t // edges : t // edges + 1, t % edges : t % edges + 128]
             same[at : at + 128, t : t + 128] = jnp.where(wide == other, 1.0, 0.0).astype(BF16)
 
-    for sl in chunks:
-        store_parts(sl.start, rest[:, sl])
-    ahead = [gather(0), gather(1)]
+    ahead = [gather(0, rp), gather(1, rp)]
     receive(0, None)
     for k in (1, 0):
         send(1, k, ahead[k] - across(k) * shrink)
-    for sl in chunks:
-        z = rest[:, sl] - mask[0:1, sl] * landed(sl) * shrink
-        fb[:, sl] = z
-        store_parts(sl.start, z)
-
     for d in range(1, size_y):
         wait_from(0, mxa, me_y, size_y, peer_y, d).wait_recv()
     mxb[me_x] = jnp.max(mxa[...], axis=0)
     for c in exchange(1, mxb, peer_x, me_x, size_x):
         c.start()
+    for sl in chunks:
+        z = rest[:, sl] - mask[0:1, sl] * landed(sl) * shrink
+        fb[:, sl] = z
+        store_parts(sl.start, z)
 
     def local_lz(here, wv):
-        rest[:, here] = mask[0:1, here] * (deg[0:1, here] * fb[:, here] - wv)
+        keep(here, mask[0:1, here] * (deg[0:1, here] * fb[:, here] - wv))
 
     multiply(local_lz, block)
-    for sl in chunks:
-        store_parts(sl.start, rest[:, sl])
-    ahead = [gather(0), gather(1)]
+    ahead = [gather(0, rp), gather(1, rp)]
     receive(1, shrink)
     for d in range(1, size_x):
         wait_from(1, mxb, me_x, size_x, peer_x, d).wait_recv()
@@ -377,16 +392,14 @@
     previous, current = fa, fb
     for app in (2, 3):
 
-        def local_next(here, wv, previous=previous, current=current):
+        def local_next(here, wv, app=app, previous=previous, current=current):
             y = current[:, here]
             lap = mask[0:1, here] * (deg[0:1, here] * y - wv)
-            rest[:, here] = twice * (lap - centre * y) - previous[:, here]
+            keep(here, twice * (lap - centre * y) - previous[:, here], app == 2)
 
         multiply(local_next, block)
         if app == 2:
-            for sl in chunks:
-                store_parts(sl.start, rest[:, sl])
-            ahead = [gather(0), gather(1)]
+            ahead = [gather(0, rp), gather(1, rp)]
         receive(app, None)
         if app == 2:
             for k in (1, 0):
@@ -398,7 +411,9 @@
             store_parts(sl.start, new)
         previous, current = current, previous
 
-    both = parts_at(0, cells)
+    filtered = pltpu.make_async_copy(vp, parts_ref, psem)
+    filtered.start()
+    both = all_parts(vp)
     full = dot(both, both, NT)
     gram = full[0:vecs, 0:vecs] + full[0:vecs, vecs:] + full[vecs:, 0:vecs] + full[vecs:, vecs:]
     gram = jnp.concatenate([gram, jnp.zeros((vecs, 128 - vecs), F32)], axis=1)
@@ -486,23 +501,35 @@
         for c in exchange(3, gr2, peer_x, me_x, size_x) + exchange(4, gfull, peer_y, me_y, size_y):
             c.wait_send()
 
-
-def finish_kernel(scale, gram_ref, parts_ref, out_ref, work, elem, inv):
-    vecs = out_ref.shape[2]
-
-    @pl.when(pl.program_id(0) == 0)
-    def _():
-        work[...] = gram_ref[...]
-        inverse_factor(work, elem, inv, scale, vecs)
-
+    filtered.wait()
+
+
+def finish_kernel(scale, gram_ref, parts_ref, out_ref, work, elem, inv, parts, result, psem, osem):
+    vecs, cells = out_ref.shape[2:]
+    fetch = pltpu.make_async_copy(parts_ref, parts, psem)
+    fetch.start()
+    work[...] = gram_ref[...]
+    inverse_factor(work, elem, inv, scale, vecs)
     hi, lo = split(inv[...])
     hi, lo = hi[:, 0:vecs], lo[:, 0:vecs]
     left = jnp.concatenate(
         [jnp.concatenate([hi, hi], axis=1), jnp.concatenate([lo, lo], axis=1)], axis=0
     )
-    right = jnp.concatenate([parts_ref[t] for t in range(parts_ref.shape[0])], axis=1)
-    got = dot(left, right)
-    out_ref[0, 0] = got[0:vecs] + got[vecs:]
+    fetch.wait()
+    blocks, chunks = parts.shape[0], osem.shape[0]
+    each, width = blocks // chunks, cells // chunks
+    writes = []
+    for q in range(chunks):
+        got = dot(left, jnp.concatenate([parts[q * each + t] for t in range(each)], axis=1))
+        result[q] = got[0:vecs] + got[vecs:]
+        writes.append(
+            pltpu.make_async_copy(
+                result.at[q], out_ref.at[0, 0, :, pl.ds(q * width, width)], osem.at[q]
+            )
+        )
+        writes[q].start()
+    for w in writes:
+        w.wait()
 
 
 def per_device(size_x, size_y, basis, block_vals, block_cols, edge_rows, live_counts):
@@ -513,12 +540,14 @@
     vmem = pltpu.VMEM
     field = vmem((vecs, cells), F32)
     scratch = [
+        vmem((blocks, 2 * vecs, block), BF16),
+        vmem((blocks, 2 * vecs, block), BF16),
         vmem((blocks, stored, block, block), F32),
         vmem((blocks, 2 * block, stored * block), BF16),
         vmem((cells, ends), BF16),
         vmem((ends, cells), BF16),
         vmem((ends, ends), BF16),
-        vmem((blocks, 16, block), BF16),
+        vmem((blocks, 8, block), F32),
         vmem((2 * vecs, ends), BF16),
         field,
         field,
@@ -533,6 +562,7 @@
         vmem((size_y, 8, 128), F32),
         vmem((size_x, 8, 128), F32),
         pltpu.SemaphoreType.DMA((blocks,)),
+        pltpu.SemaphoreType.DMA,
         pltpu.SemaphoreType.DMA((4, sides)),
         pltpu.SemaphoreType.DMA((4, sides)),
         pltpu.SemaphoreType.DMA((5, max(size_x, size_y))),
@@ -547,7 +577,7 @@
             jax.ShapeDtypeStruct((vecs // 8, 8, 128), F32),
         ],
         in_specs=[in_smem, in_smem, in_vmem, in_vmem, pl.BlockSpec(memory_space=pl.ANY)],
-        out_specs=[in_vmem, in_vmem],
+        out_specs=[pl.BlockSpec(memory_space=pl.ANY), in_vmem],
         scratch_shapes=scratch,
         compiler_params=pltpu.CompilerParams(
             collective_id=0, has_side_effects=True, vmem_limit_bytes=60 * 2**20
@@ -558,16 +588,16 @@
     return pl.pallas_call(
         lambda *refs: finish_kernel(math.sqrt(cells * size_x * size_y), *refs),
         out_shape=jax.ShapeDtypeStruct(basis.shape, F32),
-        grid=(steps,),
-        in_specs=[
-            pl.BlockSpec(gram.shape, lambda i: (0, 0, 0)),
-            pl.BlockSpec((blocks // steps, 2 * vecs, block), lambda i: (i, 0, 0)),
-        ],
-        out_specs=pl.BlockSpec((1, 1, vecs, cells // steps), lambda i: (0, 0, 0, i)),
+        in_specs=[in_vmem, pl.BlockSpec(memory_space=pl.ANY)],
+        out_specs=pl.BlockSpec(memory_space=pl.ANY),
         scratch_shapes=[
             vmem(gram.shape, F32),
             vmem((8, 8, 128), F32),
             vmem((vecs, 128), F32),
+            vmem(parts.shape, BF16),
+            vmem((steps, vecs, cells // steps), F32),
+            pltpu.SemaphoreType.DMA,
+            pltpu.SemaphoreType.DMA((steps,)),
         ],
         compiler_params=pltpu.CompilerParams(vmem_limit_bytes=60 * 2**20),
         name="factor_and_encode",

time: 62.4 us -> 60.3 us (0.966)
  Pallas kernels: 61.6 us -> 59.3 us
    pallas_call x1, Pallas kernels: 6.37 us -> 4.65 us  [per_device(): pl.pallas_call(lambda *refs: finish_kernel(math.sqrt(cells * size_x * siz...]
where the time goes in v2:
time: 60.3 us; the launch traced here: 60.1 us
  Pallas kernels  59.3 us (98%)
  between operations  0.82 us (1%)
    pallas_call x1, Pallas kernels, per_device(): pl.pallas_call(lambda *refs: filter_kernel(size_x, size_y, *refs), out_sh...  54.7 us
    pallas_call x1, Pallas kernels, per_device(): pl.pallas_call(lambda *refs: finish_kernel(math.sqrt(cells * size_x * siz...  4.65 us

profile of v2, /device:TPU:1, one launch (start us, length us, event | category | flops | bytes accessed | tf_op | source)
XLA Modules:
  0.0 60.1 jit_solution(6485134987290703155)
XLA Ops:
  0.7 54.7 %filter_and_gram.1 = (bf16[16,192,128]{2,1,0:T(8,128)(2,1)}, f32[12,8,128]{2,1,0:T(8,128)}) custom-call(s32[1,1]{1,0:T(1,128)S(6)} %copy.6.refs_0_, s32[1,5,1,16]{3,2,1,0:T(1,128)} %bitcast.1, f32[1,1,96,2048]{3,2,1,0:T(8,128)} %refs_2_.1, s32[1,1,4,256]{3,2,1,0:T(4,128)} %refs_3_.1, f32[1,1,16,5,128,128]{5,4,3,2,1,0:T(8,128)} %refs_4_.1), custom_call_target="tpu_custom_call" | custom-call | tf_op jit(solution)/shard_map/filter_and_gram/pallas_call | solution.py:573
  55.3 4.6 %factor_and_encode.1 = f32[1,1,96,2048]{3,2,1,0:T(8,128)} custom-call(f32[12,8,128]{2,1,0:T(8,128)} %get-tuple-element.7.refs_0_, bf16[16,192,128]{2,1,0:T(8,128)(2,1)} %get-tuple-element.8.refs_1_), custom_call_target="tpu_custom_call" | custom-call | tf_op jit(solution)/shard_map/factor_and_encode/pallas_call | solution.py:588

commit v3 on v2

--- a/solution.py
+++ b/solution.py
@@ -128,17 +128,17 @@
     def peer_y(d):
         return {"gx": me_x, "gy": lax.rem(me_y + d, size_y)}
 
+    fetches = [
+        pltpu.make_async_copy(vals_ref.at[0, 0, n], raw.at[n], wsem.at[n]) for n in range(blocks)
+    ]
+    for f in fetches:
+        f.start()
+
     barrier = pltpu.get_barrier_semaphore()
     for d in range(1, size_x):
         pl.semaphore_signal(barrier, inc=1, device_id=peer_x(d), device_id_type=MESH)
     for d in range(1, size_y):
         pl.semaphore_signal(barrier, inc=1, device_id=peer_y(d), device_id_type=MESH)
-
-    fetches = [
-        pltpu.make_async_copy(vals_ref.at[0, 0, n], raw.at[n], wsem.at[n]) for n in range(blocks)
-    ]
-    for f in fetches:
-        f.start()
 
     has = [me_x > 0, me_x < size_x - 1, me_y > 0, me_y < size_y - 1]
     target = [
@@ -186,16 +186,19 @@
     store_parts(0, start)
 
     step = 128
+    position = lax.broadcasted_iota(jnp.int32, (step, edges), 0).astype(F32).astype(BF16)
+    one, none = jnp.ones((step, edges), BF16), jnp.zeros((step, edges), BF16)
 
     @pl.loop(0, cells // step)
     def _(t):
         base = pl.multiple_of(t * step, step)
-        cell = lax.broadcasted_iota(jnp.int32, (step, edges), 0) + base
         for side in range(sides):
-            ends = edges_ref[0, 0, side : side + 1, :]
+            inside = edges_ref[0, 0, side : side + 1, :] - base
+            inside = jnp.where((inside >= 0) & (inside < step), inside, 255)
+            key = jnp.broadcast_to(inside.astype(F32), (step, edges)).astype(BF16)
             pick[pl.ds(base, step), side * edges : (side + 1) * edges] = jnp.where(
-                cell == ends, 1.0, 0.0
-            ).astype(BF16)
+                position == key, one, none
+            )
 
     chunk = 512
     chunks = [slice(q * chunk, (q + 1) * chunk) for q in range(cells // chunk)]
@@ -282,22 +285,35 @@
     send(0, 1, ahead)
     send(0, 0, gather(0, vp))
 
-    lane = lax.broadcasted_iota(jnp.int32, (128, 128), 1)
+    lane = lax.broadcasted_iota(jnp.int32, (128, 128), 1).astype(F32).astype(BF16)
+    zero = jnp.zeros((128, 128), BF16)
+
+    def apart(ends):
+        high = lax.shift_right_logical(ends, 7)
+        return high.astype(F32), (ends - high * 128).astype(F32)
 
     def down(at):
         side, from_edge = at // edges, at % edges
         ends = edges_ref[0, 0, side : side + 1, from_edge : from_edge + 128]
-        col = jnp.transpose(jnp.broadcast_to(ends.astype(F32), (8, 128)))[:, 0:1]
-        return jnp.broadcast_to(col, (128, 128)).astype(jnp.int32)
-
-    counts = [jnp.zeros((8, 128), F32) for _ in range(cells // 128)]
+        wide = [
+            jnp.broadcast_to(
+                jnp.transpose(jnp.broadcast_to(x, (8, 128)))[:, 0:1], (128, 128)
+            ).astype(BF16)
+            for x in apart(ends)
+        ]
+        return wide[0], wide[1], jnp.where(wide[1] == lane, jnp.ones((128, 128), BF16), zero)
+
+    counts = [jnp.zeros((16, 128), F32) for _ in range(cells // 128)]
     for at in range(0, ends_all, 128):
-        wide = down(at)
+        high, _, spot = down(at)
         flag = jnp.where(has[at // edges], 1.0, 0.0).astype(F32)
         for t in range(cells // 128):
-            hit = jnp.where(wide == lane + t * 128, 1.0, 0.0)
-            place[at : at + 128, t * 128 : (t + 1) * 128] = hit.astype(BF16)
-            counts[t] = counts[t] + flag * jnp.sum(hit.reshape(16, 8, 128), axis=0)
+            hit = jnp.where(high == jnp.full((128, 128), t, BF16), spot, zero)
+            place[at : at + 128, t * 128 : (t + 1) * 128] = hit
+            some = hit[0:16]
+            for r in range(16, 128, 16):
+                some = some + hit[r : r + 16]
+            counts[t] = counts[t] + flag * some.astype(F32)
     for t in range(cells // 128):
         deg[:, t * 128 : (t + 1) * 128] = jnp.broadcast_to(
             jnp.sum(counts[t], axis=0, keepdims=True), (8, 128)
@@ -340,10 +356,14 @@
     multiply(local_z, block)
 
     for at in range(0, ends_all, 128):
-        wide = down(at)
+        high, low, _ = down(at)
         for t in range(0, ends_all, 128):
             other = edges_ref[0, 0, t // edges : t // edges + 1, t % edges : t % edges + 128]
-            same[at : at + 128, t : t + 128] = jnp.where(wide == other, 1.0, 0.0).astype(BF16)
+            far_high, far_low = (
+                jnp.broadcast_to(x, (128, 128)).astype(BF16) for x in apart(other)
+            )
+            meet = jnp.where(low == far_low, jnp.ones((128, 128), BF16), zero)
+            same[at : at + 128, t : t + 128] = jnp.where(high == far_high, meet, zero)
 
     ahead = [gather(0, rp), gather(1, rp)]
     receive(0, None)

time: 60.3 us -> 59.9 us (level)
  no operation moved by 1% of the time
where the time goes in v3:
time: 59.9 us; the launch traced here: 59.7 us
  Pallas kernels  58.9 us (98%)
  between operations  0.82 us (1%)
    pallas_call x1, Pallas kernels, per_device(): pl.pallas_call(lambda *refs: filter_kernel(size_x, size_y, *refs), out_sh...  54.2 us
    pallas_call x1, Pallas kernels, per_device(): pl.pallas_call(lambda *refs: finish_kernel(math.sqrt(cells * size_x * siz...  4.65 us

profile of v3, /device:TPU:1, one launch (start us, length us, event | category | flops | bytes accessed | tf_op | source)
XLA Modules:
  0.0 59.7 jit_solution(14612810188701360947)
XLA Ops:
  0.7 54.2 %filter_and_gram.1 = (bf16[16,192,128]{2,1,0:T(8,128)(2,1)}, f32[12,8,128]{2,1,0:T(8,128)}) custom-call(s32[1,1]{1,0:T(1,128)S(6)} %copy.6.refs_0_, s32[1,5,1,16]{3,2,1,0:T(1,128)} %bitcast.1, f32[1,1,96,2048]{3,2,1,0:T(8,128)} %refs_2_.1, s32[1,1,4,256]{3,2,1,0:T(4,128)} %refs_3_.1, f32[1,1,16,5,128,128]{5,4,3,2,1,0:T(8,128)} %refs_4_.1), custom_call_target="tpu_custom_call" | custom-call | tf_op jit(solution)/shard_map/filter_and_gram/pallas_call | solution.py:593
  54.9 4.6 %factor_and_encode.1 = f32[1,1,96,2048]{3,2,1,0:T(8,128)} custom-call(f32[12,8,128]{2,1,0:T(8,128)} %get-tuple-element.7.refs_0_, bf16[16,192,128]{2,1,0:T(8,128)(2,1)} %get-tuple-element.8.refs_1_), custom_call_target="tpu_custom_call" | custom-call | tf_op jit(solution)/shard_map/factor_and_encode/pallas_call | solution.py:608

commit v4 on v3

--- a/solution.py
+++ b/solution.py
@@ -108,6 +108,7 @@
     gr2,
     wsem,
     psem,
+    bsem,
     hs,
     hr,
     cs,
@@ -128,6 +129,8 @@
     def peer_y(d):
         return {"gx": me_x, "gy": lax.rem(me_y + d, size_y)}
 
+    load = pltpu.make_async_copy(basis_ref.at[0, 0], rest, bsem)
+    load.start()
     fetches = [
         pltpu.make_async_copy(vals_ref.at[0, 0, n], raw.at[n], wsem.at[n]) for n in range(blocks)
     ]
@@ -181,10 +184,6 @@
     def all_parts(src):
         return jnp.concatenate([src[t] for t in range(blocks)], axis=1)
 
-    start = basis_ref[0, 0] * mask[0:1, :]
-    fa[...] = start
-    store_parts(0, start)
-
     step = 128
     position = lax.broadcasted_iota(jnp.int32, (step, edges), 0).astype(F32).astype(BF16)
     one, none = jnp.ones((step, edges), BF16), jnp.zeros((step, edges), BF16)
@@ -199,6 +198,11 @@
             pick[pl.ds(base, step), side * edges : (side + 1) * edges] = jnp.where(
                 position == key, one, none
             )
+
+    load.wait()
+    start = rest[...] * mask[0:1, :]
+    fa[...] = start
+    store_parts(0, start)
 
     chunk = 512
     chunks = [slice(q * chunk, (q + 1) * chunk) for q in range(cells // chunk)]
@@ -583,12 +587,14 @@
         vmem((size_x, 8, 128), F32),
         pltpu.SemaphoreType.DMA((blocks,)),
         pltpu.SemaphoreType.DMA,
+        pltpu.SemaphoreType.DMA,
         pltpu.SemaphoreType.DMA((4, sides)),
         pltpu.SemaphoreType.DMA((4, sides)),
         pltpu.SemaphoreType.DMA((5, max(size_x, size_y))),
         pltpu.SemaphoreType.DMA((5, max(size_x, size_y))),
     ]
     in_vmem = pl.BlockSpec(memory_space=vmem)
+    in_hbm = pl.BlockSpec(memory_space=pl.ANY)
     in_smem = pl.BlockSpec(memory_space=pltpu.SMEM)
     parts, gram = pl.pallas_call(
         lambda *refs: filter_kernel(size_x, size_y, *refs),
@@ -596,8 +602,8 @@
             jax.ShapeDtypeStruct((blocks, 2 * vecs, block), BF16),
             jax.ShapeDtypeStruct((vecs // 8, 8, 128), F32),
         ],
-        in_specs=[in_smem, in_smem, in_vmem, in_vmem, pl.BlockSpec(memory_space=pl.ANY)],
-        out_specs=[pl.BlockSpec(memory_space=pl.ANY), in_vmem],
+        in_specs=[in_smem, in_smem, in_hbm, in_vmem, in_hbm],
+        out_specs=[in_hbm, in_vmem],
         scratch_shapes=scratch,
         compiler_params=pltpu.CompilerParams(
             collective_id=0, has_side_effects=True, vmem_limit_bytes=60 * 2**20

time: 59.9 us -> 59.4 us (level)
  no operation moved by 1% of the time
where the time goes in v4:
time: 59.4 us; the launch traced here: 59.2 us
  Pallas kernels  58.4 us (98%)
  between operations  0.82 us (1%)
    pallas_call x1, Pallas kernels, per_device(): pl.pallas_call(lambda *refs: filter_kernel(size_x, size_y, *refs), out_sh...  53.8 us
    pallas_call x1, Pallas kernels, per_device(): pl.pallas_call(lambda *refs: finish_kernel(math.sqrt(cells * size_x * siz...  4.65 us

profile of v4, /device:TPU:1, one launch (start us, length us, event | category | flops | bytes accessed | tf_op | source)
XLA Modules:
  0.0 59.2 jit_solution(17094080824961585626)
XLA Ops:
  0.7 53.8 %filter_and_gram.1 = (bf16[16,192,128]{2,1,0:T(8,128)(2,1)}, f32[12,8,128]{2,1,0:T(8,128)}) custom-call(s32[1,1]{1,0:T(1,128)S(6)} %copy.6.refs_0_, s32[1,5,1,16]{3,2,1,0:T(1,128)} %bitcast.1, f32[1,1,96,2048]{3,2,1,0:T(8,128)} %refs_2_.1, s32[1,1,4,256]{3,2,1,0:T(4,128)} %refs_3_.1, f32[1,1,16,5,128,128]{5,4,3,2,1,0:T(8,128)} %refs_4_.1), custom_call_target="tpu_custom_call" | custom-call | tf_op jit(solution)/shard_map/filter_and_gram/pallas_call | solution.py:599
  54.4 4.6 %factor_and_encode.1 = f32[1,1,96,2048]{3,2,1,0:T(8,128)} custom-call(f32[12,8,128]{2,1,0:T(8,128)} %get-tuple-element.7.refs_0_, bf16[16,192,128]{2,1,0:T(8,128)(2,1)} %get-tuple-element.8.refs_1_), custom_call_target="tpu_custom_call" | custom-call | tf_op jit(solution)/shard_map/factor_and_encode/pallas_call | solution.py:614
